TPU v7x, 32 devices: a whole 2x2x4 slice. The times are simulated.
32 devices in a mesh: row: 16 (over z, y, x), col: 2 (over core).
Axes of the slice: x: 2, y: 2, z: 4, core: 2. Of those that a mesh axis runs over, the one named last changes fastest.
Arguments:
- root_cov: float32 [6144, 6144], P('row', 'col'), as said below
- structure: int32 [16], replicated, may hold values from 0 to 47
- child_factor: float32 [2048, 4096], P('row', 'col'), may hold values from -0.9 to 0.9
- child_diag: float32 [4096, 4096], P('row', 'col'), may hold values from -6 to 6
Outputs:
- cross_cov: float32 [2048, 4096], P('row', 'col')
- child_cov: float32 [4096, 4096], P('row', 'col')
Inputs may be any that keep to these rules, and one draw needn't show every extreme that they name: root_cov is exactly symmetric and positive definite; its off-diagonal entries are small against its diagonal, which is about 1.5 times the product of a row scale and a column scale.
All inputs are finite; a program needn't handle non-finite values.
Results may differ from a plain program's by a relative error of at most 0.000078.
Values sent between devices are 32-bit elements; how exact they have to be, the bound alone decides.
A program may use at most 128 MiB of HBM per device.

v0:
```python
import jax
import jax.numpy as jnp
from jax import lax
from jax.sharding import PartitionSpec as P

BLK = 128


def contract_rows(first_mat, second_mat):
    return lax.dot_general(
        first_mat,
        second_mat,
        (((0,), (0,)), ((), ())),
        precision=lax.Precision.HIGHEST,
        preferred_element_type=jnp.float32,
    )


def per_device(root_cov, structure, child_factor, child_diag):
    rows_dev = root_cov.shape[0]
    offsets = lax.iota(jnp.int32, BLK)
    struct_rows = (structure[:, None] * BLK + offsets[None, :]).reshape(-1)
    row_index = lax.axis_index("row")
    global_rows = row_index * rows_dev + lax.iota(jnp.int32, rows_dev)
    tile_index = global_rows // BLK
    rank_count = jnp.sum((structure[None, :] < tile_index[:, None]).astype(jnp.int32), axis=1)
    member = jnp.any(structure[None, :] == tile_index[:, None], axis=1)
    position = rank_count * BLK + global_rows % BLK
    shard_piece = lax.all_gather(root_cov, "col", axis=1, tiled=True)
    local_index = struct_rows
    inside = (local_index >= 0) & (local_index < shard_piece.shape[1])
    taken_rows = jnp.take(shard_piece, jnp.clip(local_index, 0, shard_piece.shape[1] - 1), axis=1)
    picked = jnp.where(inside[None, :], taken_rows, 0.0)
    shard_piece = lax.all_gather(child_factor, "row", axis=0, tiled=True)
    local_index = position
    inside = member & (local_index >= 0) & (local_index < shard_piece.shape[0])
    taken_rows = jnp.take(shard_piece, jnp.clip(local_index, 0, shard_piece.shape[0] - 1), axis=0)
    spread = jnp.where(inside[:, None], taken_rows, 0.0)
    cross_cov = lax.psum_scatter(
        -contract_rows(picked, spread), "row", scatter_dimension=0, tiled=True
    )
    factor_rows = lax.all_gather(child_factor, "col", axis=1, tiled=True)
    child_cov = child_diag + lax.psum_scatter(
        -contract_rows(factor_rows, cross_cov), "row", scatter_dimension=0, tiled=True
    )
    return (cross_cov, child_cov)


def solution(mesh):
    return jax.shard_map(
        per_device,
        mesh=mesh,
        in_specs=(P("row", "col"), P(), P("row", "col"), P("row", "col")),
        out_specs=(P("row", "col"), P("row", "col")),
        check_vma=False,
    )
```

profile of v0, /device:TPU:0, one launch (start us, length us, event | category | flops | bytes accessed | tf_op | source)
XLA Modules:
  0.0 1354.2 jit_solution(650984448894436016)
XLA Ops:
  7.2 0.0 all-gather.4.cloned.1.call-start
  7.2 6.1 copy.12
  13.3 0.0 all-gather.6.cloned.1.call-start
  13.4 0.7 all-gather.6.cloned.1.call-update
  14.1 0.0 all-gather.8.cloned.1.call-start
  14.1 0.7 all-gather.8.cloned.1.call-update
  14.8 0.0 reduce-scatter.3.cloned.1.call-start
  14.9 0.1 convert_reduce_fusion
  15.0 0.1 compare_reduce_fusion
  15.1 0.1 compare_and_fusion
  15.2 0.1 fusion.16
  15.4 0.1 fusion.12
  15.5 22.6 %all-gather.4.cloned.1.call-done = f32[384,6144]{0,1:T(8,128)} async-done(((f32[384,3072]{0,1:T(8,128)}), f32[384,6144]{0,1:T(8,128)}) %all-gather.4.cloned.1.call-update) | async-done | bytes 9437200 | tf_op jit(solution)/shard_map/all_gather | solution.py:29
  38.0 10.9 gather_fusion
  48.9 184.7 %all-gather.6.cloned.1.call-done = f32[2048,2048]{1,0:T(8,128)} async-done(((f32[128,2048]{1,0:T(8,128)}), f32[2048,2048]{1,0:T(8,128)}) %all-gather.6.cloned.1.call-update) | async-done | bytes 16777232 | tf_op jit(solution)/shard_map/all_gather | solution.py:34
  233.6 10.9 gather_fusion.1
  244.6 31.4 %convolution_negate_fusion = f32[2048,2048]{1,0:T(8,128)} fusion(f32[2048,384]{1,0:T(8,128)S(1)} %gather_fusion, f32[384,2048]{1,0:T(8,128)} %gather_fusion.1, pred[384]{0:T(512)(128)(4,1)S(1)} %compare_and_fusion.1, pred[384]{0:T(512)(128)(4,1)S(1)} %get-tuple-element.8, pred[2048]{0:T(1024)(128)(4,1)S(1)} %fusion.16, pred[2048]{0:T(1024)(128)(4,1)S(1)} %compare_and_fusion), kind=kOutput, calls=%fused_computation.3 | convolution fusion | flops 19334692864 | bytes 23073536 | tf_op jit(solution)/shard_map/dot_general | solution.py:10
  275.9 0.2 reduce-scatter.5.cloned.1.call-start
  276.2 344.4 %reduce-scatter.3.cloned.1.call-done = f32[128,2048]{1,0:T(8,128)} async-done(((f32[2048,2048]{1,0:T(8,128)}), f32[128,2048]{1,0:T(8,128)}) %reduce-scatter.3.cloned.1.call-update) | async-done | bytes 1048592 | tf_op jit(solution)/shard_map/reduce_scatter | solution.py:39
  620.6 31.7 %negate_bitcast_fusion = f32[4096,2048]{0,1:T(8,128)} fusion(f32[128,2048]{1,0:T(8,128)} %reduce-scatter.3.cloned.1.call-done, f32[128,4096]{1,0:T(8,128)} %all-gather.8.cloned.1.call-done), kind=kOutput, calls=%fused_computation.2 | convolution fusion | flops 12893290496 | bytes 36700160 | tf_op jit(solution)/shard_map/dot_general | solution.py:10
  652.4 1.9 copy.13
  654.3 687.3 %reduce-scatter.5.cloned.1.call-done = f32[256,2048]{0,1:T(8,128)} async-done(((f32[4096,2048]{0,1:T(8,128)}), f32[256,2048]{0,1:T(8,128)}) %reduce-scatter.5.cloned.1.call-update) | async-done | bytes 2097168 | tf_op jit(solution)/shard_map/reduce_scatter | solution.py:43
  1341.6 3.2 add.152
  1344.8 2.9 copy.14
  (15 shorter events, 0.2 us)
Async XLA Ops:
  7.2 30.9 %all-gather.4.cloned.1.call-start = ((), (), s32[]{:S(2)}) async-start(), calls=%async_computation.2 | async-start | bytes 14155776 | tf_op jit(solution)/shard_map/all_gather | solution.py:29
  13.3 1.6 copy-start
  13.3 220.3 %all-gather.6.cloned.1.call-start = ((), (), s32[]{:S(2)}) async-start(), calls=%async_computation.3 | async-start | bytes 17825792 | tf_op jit(solution)/shard_map/all_gather | solution.py:34
  14.1 262.1 %all-gather.8.cloned.1.call-start = ((), (), s32[]{:S(2)}) async-start(), calls=%async_computation.5 | async-start | bytes 3145728 | tf_op jit(solution)/shard_map/all_gather | solution.py:42
  14.8 605.8 %reduce-scatter.3.cloned.1.call-start = ((), (), s32[]{:S(2)}) async-start(), calls=%async_computation.4 | async-start | bytes 17825792 | tf_op jit(solution)/shard_map/reduce_scatter | solution.py:39
  275.9 1065.6 %reduce-scatter.5.cloned.1.call-start = ((), (), s32[]{:S(2)}) async-start(), calls=%async_computation.6 | async-start | bytes 35651584 | tf_op jit(solution)/shard_map/reduce_scatter | solution.py:43
Sparse Core Ops, SparseCore 0:
  13.5 24.5 all-gather.3
  40.8 192.7 all-gather.5
  235.2 8.7 all-gather.7
  276.1 344.4 reduce-scatter.2
  652.5 689.0 reduce-scatter.4
where the time goes:
time: 1360 us; the launch traced here: 1350 us
  waiting for transfers between devices  1240 us (91%)
  matrix products  63.1 us (5%)
  local copies, waits for them, and re-layouts  32.7 us (2%)
  between operations  13.9 us (1%)
    reduce_scatter x1, waiting for transfers between devices, per_device(): lax.psum_scatter(-contract_rows(factor_rows, cross_cov), 'row', scatter_d...  687 us
    reduce_scatter x1, waiting for transfers between devices, per_device(): lax.psum_scatter(-contract_rows(picked, spread), 'row', scatter_dimension...  344 us
    all_gather x1, waiting for transfers between devices, per_device(): shard_piece = lax.all_gather(child_factor, 'row', axis=0, tiled=True)  185 us
    dot_general x2, matrix products, contract_rows(): lax.dot_general(first_mat, second_mat, (((0,), (0,)), ((), ())), precisio...  63.1 us
  transfers between devices with their start and end apart: 5, of which 4 were waited for; matrix products, arithmetic and copies ran while one was open for 4% of the time, Pallas kernels for 0%

commit v1 on v0

v1 whole, which is shorter than its diff:
```python
import jax
import jax.numpy as jnp
from jax import lax
from jax.sharding import Mesh, PartitionSpec as P

BLK = 128
NB = 4
HIGH = lax.Precision.HIGH


def contract_rows(first_mat, second_mat):
    return lax.dot_general(
        first_mat,
        second_mat,
        (((0,), (0,)), ((), ())),
        precision=HIGH,
        preferred_element_type=jnp.float32,
    )


def plain_device(root_cov, structure, child_factor, child_diag):
    rows_dev = root_cov.shape[0]
    offsets = lax.iota(jnp.int32, BLK)
    struct_rows = (structure[:, None] * BLK + offsets[None, :]).reshape(-1)
    row_index = lax.axis_index("row")
    global_rows = row_index * rows_dev + lax.iota(jnp.int32, rows_dev)
    tile_index = global_rows // BLK
    rank_count = jnp.sum((structure[None, :] < tile_index[:, None]).astype(jnp.int32), axis=1)
    member = jnp.any(structure[None, :] == tile_index[:, None], axis=1)
    position = rank_count * BLK + global_rows % BLK
    picked = jnp.take(lax.all_gather(root_cov, "col", axis=1, tiled=True), struct_rows, axis=1)
    factor = lax.all_gather(child_factor, "row", axis=0, tiled=True)
    rows = jnp.take(factor, jnp.clip(position, 0, factor.shape[0] - 1), axis=0)
    spread = jnp.where(member[:, None], rows, 0.0)
    cross_cov = lax.psum_scatter(
        -contract_rows(picked, spread), "row", scatter_dimension=0, tiled=True
    )
    factor_rows = lax.all_gather(child_factor, "col", axis=1, tiled=True)
    child_cov = child_diag + lax.psum_scatter(
        -contract_rows(factor_rows, cross_cov), "row", scatter_dimension=0, tiled=True
    )
    return (cross_cov, child_cov)


def select_quarter(root_cov, structure, z, b, c):
    tiles_dev = root_cov.shape[0] // BLK
    col_tiles = root_cov.shape[1] // BLK
    kb = structure.shape[0]
    parts = []
    for j in range(kb):
        at = structure[j] - c * col_tiles
        inside = (at >= 0) & (at < col_tiles)
        start = jnp.clip(at, 0, col_tiles - 1) * BLK
        piece = lax.dynamic_slice(root_cov, (0, start), (root_cov.shape[0], BLK))
        parts.append(jnp.where(inside, piece, 0.0))
    picked = jnp.concatenate(parts, axis=1)
    half = lax.psum_scatter(picked, "col", scatter_dimension=1, tiled=True)
    first = (z * NB + b) * tiles_dev
    parts = []
    for j in range(kb):
        at = structure[j] - first
        inside = (at >= 0) & (at < tiles_dev)
        start = jnp.clip(at, 0, tiles_dev - 1) * BLK
        piece = lax.dynamic_slice(half, (start, 0), (BLK, half.shape[1]))
        parts.append(jnp.where(inside, piece, 0.0))
    full = jnp.concatenate(parts, axis=0)
    mine = lax.psum_scatter(full, ("z", "b"), scatter_dimension=0, tiled=True)
    quarter = lax.all_gather(mine, "z", axis=0, tiled=True)
    return lax.all_gather(quarter, "col", axis=1, tiled=True)


def grouped_device(root_cov, structure, child_factor, child_diag):
    z, b, c = lax.axis_index("z"), lax.axis_index("b"), lax.axis_index("col")
    nz = lax.axis_size("z")
    depth, width = child_factor.shape
    k = depth * nz * NB
    zh = nz // 2
    sub = width // (zh * NB)
    f4 = child_factor.reshape(depth, zh, NB, sub)
    f_i = lax.all_to_all(f4, "b", split_axis=2, concat_axis=0, tiled=True)
    f_i = lax.all_gather(f_i.reshape(NB * depth, zh * sub), "z", axis=0, tiled=True)
    quarter = select_quarter(root_cov, structure, z, b, c)
    own = lax.dynamic_slice(f_i, (0, (z % zh) * sub), (k, sub))
    other = lax.ppermute(own, "col", [(0, 1), (1, 0)])
    own = jnp.where(c == z // zh, own, other)
    hs = sub // 2
    own = lax.dynamic_slice(own, (0, c * hs), (k, hs))
    f_j = lax.all_gather(own, "b", axis=1, tiled=True)
    x = -jnp.dot(quarter, f_j, precision=HIGH, preferred_element_type=jnp.float32)
    x3 = x.reshape(nz, depth, NB * hs)
    x_all = lax.all_gather(x3, "b", axis=1, tiled=False).reshape(k, NB * hs)
    x_all = lax.all_gather(x_all, "col", axis=0, tiled=False)
    out = lax.dot_general(
        x_all, f_i, (((1,), (0,)), ((), ())), precision=HIGH,
        preferred_element_type=jnp.float32,
    )
    out = out.reshape(2, NB, hs, zh * sub)
    out = lax.all_to_all(out, "b", split_axis=1, concat_axis=1, tiled=True)
    out = out.reshape(2, NB, hs, zh, sub).transpose(0, 2, 3, 1, 4).reshape(2 * hs, width)
    child_cov = child_diag - out
    y = lax.all_to_all(x3, "z", split_axis=0, concat_axis=0, tiled=True)
    y = y.reshape(2, zh, depth, NB, hs)
    y = lax.all_to_all(y, "col", split_axis=0, concat_axis=0, tiled=True)
    cross_cov = y.transpose(2, 1, 3, 0, 4).reshape(depth, width)
    return (cross_cov, child_cov)


def solution(mesh):
    rows, cols = mesh.shape["row"], mesh.shape["col"]
    if cols == 2 and rows == 4 * NB:
        split = Mesh(mesh.devices.reshape(rows // NB, NB, cols), ("z", "b", "col"))
        spec = P(("z", "b"), "col")
        return jax.shard_map(
            grouped_device, mesh=split, in_specs=(spec, P(), spec, spec),
            out_specs=(spec, spec), check_vma=False,
        )
    spec = P("row", "col")
    return jax.shard_map(
        plain_device, mesh=mesh, in_specs=(spec, P(), spec, spec),
        out_specs=(spec, spec), check_vma=False,
    )
```

time: 1360 us -> 593 us (0.44)
  waiting for transfers between devices: 1240 us -> 386 us
  blocking collectives: 0 us -> 72.9 us
  matrix products: 63.1 us -> 18.3 us
  other arithmetic: 3.7 us -> 39 us
  between operations: 13.9 us -> 36.3 us
    reduce_scatter x2, waiting for transfers between devices: 1030 us -> 200 us  [the longest x1 197 us: select_quarter(): mine = lax.psum_scatter(full, ('z', 'b'), scatter_dimension=0, tiled=True)]
    all_to_all x0 -> x2, blocking collectives: none -> 72.9 us  [the longest x1 42.9 us: grouped_device(): f_i = lax.all_to_all(f4, 'b', split_axis=2, concat_axis=0, tiled=True)]
    all_gather x3 -> x6, waiting for transfers between devices: 207 us -> 160 us  [the longest x1 53.8 us: grouped_device(): x_all = lax.all_gather(x3, 'b', axis=1, tiled=False).reshape(k, NB * hs)]
    dot_general x2, matrix products: 63.1 us -> 18.3 us  [the longest x1 10.4 us: grouped_device(): lax.dot_general(x_all, f_i, (((1,), (0,)), ((), ())), precision=HIGH, pre...]
    unnamed x0 -> x30, other arithmetic: none -> 31.2 us
    gather x2 -> x0, local copies, waits for them, and re-layouts: 21.8 us -> none  [the longest x1 10.9 us: per_device(): jnp.take(shard_piece, jnp.clip(local_index, 0, shard_piece.shape[0] - 1),...]
    all_to_all x0 -> x2, waiting for transfers between devices: none -> 21.5 us  [the longest x1 21.5 us: grouped_device(): out = lax.all_to_all(out, 'b', split_axis=1, concat_axis=1, tiled=True)]
  transfers between devices with their start and end apart: 5 -> 11, of which waited for: 4 -> 8; matrix products, arithmetic and copies ran while one was open for 4% -> 4% of each run, Pallas kernels for 0% -> 0%
where the time goes in v1:
time: 593 us; the launch traced here: 591 us
  waiting for transfers between devices  386 us (65%)
  blocking collectives  72.9 us (12%)
  other arithmetic  39 us (7%)
  between operations  36.3 us (6%)
  local copies, waits for them, and re-layouts  30.8 us (5%)
  matrix products  18.3 us (3%)
  starting transfers between devices  7.78 us (1%)
    reduce_scatter x1, waiting for transfers between devices, select_quarter(): mine = lax.psum_scatter(full, ('z', 'b'), scatter_dimension=0, tiled=True)  197 us
    all_gather x1, waiting for transfers between devices, grouped_device(): x_all = lax.all_gather(x3, 'b', axis=1, tiled=False).reshape(k, NB * hs)  53.8 us
    all_gather x1, waiting for transfers between devices, grouped_device(): f_j = lax.all_gather(own, 'b', axis=1, tiled=True)  53.6 us
    all_to_all x1, blocking collectives, grouped_device(): f_i = lax.all_to_all(f4, 'b', split_axis=2, concat_axis=0, tiled=True)  42.9 us
    all_gather x1, waiting for transfers between devices, select_quarter(): quarter = lax.all_gather(mine, 'z', axis=0, tiled=True)  36.9 us
    unnamed x30, other arithmetic  31.2 us
    all_to_all x1, blocking collectives, grouped_device(): y = lax.all_to_all(x3, 'z', split_axis=0, concat_axis=0, tiled=True)  30 us
    all_to_all x1, waiting for transfers between devices, grouped_device(): out = lax.all_to_all(out, 'b', split_axis=1, concat_axis=1, tiled=True)  21.5 us
  transfers between devices with their start and end apart: 11, of which 8 were waited for; matrix products, arithmetic and copies ran while one was open for 4% of the time, Pallas kernels for 0%

profile of v1, /device:TPU:0, one launch (start us, length us, event | category | flops | bytes accessed | tf_op | source)
XLA Modules:
  0.0 591.1 jit_solution(2292876273795410014)
XLA Ops:
  8.0 2.0 fusion.2
  47.6 3.4 reduce-scatter.3.cloned.1.call-done
  51.0 2.0 select_dynamic-update-slice_fusion.15
  53.1 1.9 select_dynamic-update-slice_fusion.14
  71.4 42.9 %all_to_all.30 = f32[128,2,4,256]{3,1,0,2:T(2,128)S(1)} all-to-all(f32[128,2,4,256]{3,1,0,2:T(2,128)S(1)} %copy.14), channel_id=1, replica_groups=mesh['z'=4,'b'=4,'col'=2] {'b'}, dimensions={2} | all-to-all | bytes 2097152 | tf_op jit(solution)/shard_map/all_to_all | solution.py:80
  115.4 197.1 %reduce-scatter.5.cloned.1.call-done = f32[128,1024]{1,0:T(8,128)} async-done(((f32[2048,1024]{1,0:T(8,128)}), f32[128,1024]{1,0:T(8,128)}) %reduce-scatter.5.cloned.1.call-update) | async-done | bytes 524304 | tf_op jit(solution)/shard_map/reduce_scatter | solution.py:67
  314.4 4.3 collective-permute-done
  318.7 2.8 dynamic-slice_select_fusion
  321.5 36.9 %all-gather.7.cloned.1.call-done = f32[512,1024]{1,0:T(8,128)} async-done(((f32[128,1024]{1,0:T(8,128)}), f32[512,1024]{1,0:T(8,128)}) %all-gather.7.cloned.1.call-update) | async-done | bytes 2097168 | tf_op jit(solution)/shard_map/all_gather | solution.py:68
  358.5 53.6 %all-gather.13.cloned.1.call-done = f32[2048,512]{1,0:T(8,128)} async-done(((f32[2048,128]{1,0:T(8,128)}), f32[2048,512]{1,0:T(8,128)}) %all-gather.13.cloned.1.call-update) | async-done | bytes 4194320 | tf_op jit(solution)/shard_map/all_gather | solution.py:88
  412.1 15.2 %all-gather.9.cloned.1.call-done = f32[512,2048]{1,0:T(8,128)} async-done(((f32[512,1024]{1,0:T(8,128)}), f32[512,2048]{1,0:T(8,128)}) %all-gather.9.cloned.1.call-update) | async-done | bytes 4194320 | tf_op jit(solution)/shard_map/all_gather | solution.py:69
  427.3 7.9 %convolution_negate_fusion = f32[512,512]{1,0:T(8,128)} fusion(f32[512,2048]{1,0:T(8,128)} %all-gather.9.cloned.1.call-done, f32[2048,512]{1,0:T(8,128)} %all-gather.13.cloned.1.call-done), kind=kOutput, calls=%fused_computation.2 | convolution fusion | flops 3221487616 | bytes 9437184 | tf_op jit(solution)/shard_map/dot_general | solution.py:89
  435.3 53.8 %all-gather.15.cloned.1.call-done = f32[4,4,128,512]{3,2,0,1:T(8,128)} async-done(((f32[4,1,128,512]{3,2,0,1:T(8,128)}), f32[4,4,128,512]{3,2,0,1:T(8,128)}) %all-gather.15.cloned.1.call-update) | async-done | bytes 4194320 | tf_op jit(solution)/shard_map/all_gather | solution.py:91
  489.1 4.7 copy.18
  495.4 30.0 %all_to_all.31 = f32[4,128,512]{1,2,0:T(8,128)S(1)} all-to-all(f32[4,128,512]{1,2,0:T(8,128)S(1)} %copy.15), channel_id=1, replica_groups=mesh['z'=4,'b'=4,'col'=2] {'z'}, dimensions={0} | all-to-all | bytes 2097152 | tf_op jit(solution)/shard_map/all_to_all | solution.py:101
  526.7 3.8 all-to-all-start.2
  530.5 10.4 %fusion = f32[2,512,512]{2,1,0:T(8,128)S(1)} fusion(f32[2,2048,512]{2,1,0:T(8,128)} %all-gather.17.cloned.1.call-done, f32[2048,512]{1,0:T(8,128)} %all-gather.11.cloned.1.call-done), kind=kOutput, calls=%fused_computation | convolution fusion | flops 6442450944 | bytes 14680064 | tf_op jit(solution)/shard_map/dot_general | solution.py:93
  542.5 3.6 all-to-all-start.3
  547.6 2.5 copy.22
  550.1 21.5 %all-to-all-done.3 = f32[2,4,128,512]{3,2,0,1:T(8,128)S(1)} async-done(((f32[2,4,128,512]{3,2,0,1:T(8,128)}), f32[2,4,128,512]{3,2,0,1:T(8,128)S(1)}, u32[]{:S(2)}, u32[]{:S(2)}) %all-to-all-start.3) | async-done | bytes 2097184 | tf_op jit(solution)/shard_map/all_to_all | solution.py:98
  571.6 2.3 reshape.35
  574.0 4.3 copy.21
  578.3 2.3 reshape.36
  580.6 3.2 sub.136
  (66 shorter events, 42.4 us)
Async XLA Ops:
  8.0 43.0 %reduce-scatter.3.cloned.1.call-start = ((), (), s32[]{:S(2)}) async-start(), calls=%async_computation.6 | async-start | bytes 4718592 | tf_op jit(solution)/shard_map/reduce_scatter | solution.py:57
  35.6 1.6 copy-start.2
  37.3 275.2 %reduce-scatter.5.cloned.1.call-start = ((), (), s32[]{:S(2)}) async-start(), calls=%async_computation.7 | async-start | bytes 8912896 | tf_op jit(solution)/shard_map/reduce_scatter | solution.py:67
  51.0 7.7 %copy-start = (f32[384,1024]{1,0:T(8,128)S(1)}, f32[384,1024]{1,0:T(8,128)}, u32[]{:S(2)}) copy-start(f32[384,1024]{1,0:T(8,128)} %reduce-scatter.3.cloned.1.call-done) | copy-start | bytes 4718596
  68.9 1.2 copy-start.3
  69.0 243.6 %all-gather.11.cloned.1.call-start = ((), (), s32[]{:S(2)}) async-start(), calls=%async_computation.10 | async-start | bytes 5242880 | tf_op jit(solution)/shard_map/all_gather | solution.py:81
  115.4 243.1 %all-gather.7.cloned.1.call-start = ((), (), s32[]{:S(2)}) async-start(), calls=%async_computation.8 | async-start | bytes 2621440 | tf_op jit(solution)/shard_map/all_gather | solution.py:68
  312.5 99.6 %all-gather.13.cloned.1.call-start = ((), (), s32[]{:S(2)}) async-start(), calls=%async_computation.11 | async-start | bytes 5242880 | tf_op jit(solution)/shard_map/all_gather | solution.py:88
  314.3 4.4 collective-permute-start
  321.5 105.9 %all-gather.9.cloned.1.call-start = ((), (), s32[]{:S(2)}) async-start(), calls=%async_computation.9 | async-start | bytes 6291456 | tf_op jit(solution)/shard_map/all_gather | solution.py:69
  358.5 130.6 %all-gather.15.cloned.1.call-start = ((), (), s32[]{:S(2)}) async-start(), calls=%async_computation.12 | async-start | bytes 5242880 | tf_op jit(solution)/shard_map/all_gather | solution.py:91
  435.3 95.3 %all-gather.17.cloned.1.call-start = ((), (), s32[]{:S(2)}) async-start(), calls=%async_computation.13 | async-start | bytes 12582912 | tf_op jit(solution)/shard_map/all_gather | solution.py:92
  493.9 1.2 copy-start.1
  526.7 15.7 %all-to-all-start.2 = ((f32[2,2,128,4,128]{4,3,1,2,0:T(4,128)}), f32[2,2,128,4,128]{4,3,1,2,0:T(4,128)S(1)}, u32[]{:S(2)}, u32[]{:S(2)}) async-start(f32[2,2,128,4,128]{4,3,1,2,0:T(4,128)} %copy.16), calls=%async_computation.4 | async-start | bytes 2097152 | tf_op jit(solution)/shard_map/all_to_all | solution.py:103
  542.5 29.2 %all-to-all-start.3 = ((f32[2,4,128,512]{3,2,0,1:T(8,128)}), f32[2,4,128,512]{3,2,0,1:T(8,128)S(1)}, u32[]{:S(2)}, u32[]{:S(2)}) async-start(f32[2,4,128,512]{3,2,0,1:T(8,128)} %copy.20), calls=%async_computation.5 | async-start | bytes 4194304 | tf_op jit(solution)/shard_map/all_to_all | solution.py:98
Sparse Core Ops, SparseCore 0:
  37.4 13.6 reduce-scatter.2
  69.1 243.3 reduce-scatter.4
  494.0 19.8 all-gather.16
Sparse Core Ops, SparseCore 1:
  115.5 94.5 all-gather.10
  312.6 45.8 all-gather.6
  360.9 51.2 all-gather.12
  413.7 13.5 all-gather.8
  435.4 53.7 all-gather.14

commit v2 on v1

--- a/solution.py
+++ b/solution.py
@@ -1,11 +1,14 @@
 import jax
 import jax.numpy as jnp
 from jax import lax
+from jax.experimental import pallas as pl
+from jax.experimental.pallas import tpu as pltpu
 from jax.sharding import Mesh, PartitionSpec as P
 
 BLK = 128
 NB = 4
 HIGH = lax.Precision.HIGH
+MESH = pl.DeviceIdType.MESH
 
 
 def contract_rows(first_mat, second_mat):
@@ -42,7 +45,181 @@
     return (cross_cov, child_cov)
 
 
-def select_quarter(root_cov, structure, z, b, c):
+def gather_kernel(f_ref, a_ref, fi, fj, s, slo, loc, ssem, rp, rplane, rj, rs, rsib, rlo):
+    z, b, c = lax.axis_index("z"), lax.axis_index("b"), lax.axis_index("col")
+    low, high = z > 0, z < 3
+    home = c == z // 2
+    peers = [lax.rem(b + d, NB) for d in range(NB)]
+    sources = [lax.rem(b + NB - d, NB) for d in range(NB)]
+
+    barrier = pltpu.get_barrier_semaphore()
+
+    def greet(zz, bb, cc):
+        pl.semaphore_signal(
+            barrier, inc=1, device_id={"z": zz, "b": bb, "col": cc}, device_id_type=MESH
+        )
+
+    for d in range(NB):
+        if d:
+            greet(z, peers[d], c)
+        greet(z, peers[d], 1 - c)
+    pl.when(low)(lambda: greet(z - 1, b, c))
+    pl.when(high)(lambda: greet(z + 1, b, c))
+    pl.semaphore_wait(barrier, 2 * NB - 1 + low.astype(jnp.int32) + high.astype(jnp.int32))
+
+    sent = []
+
+    def send(cond, src, dst, rsem, zz, bb, cc):
+        at = len(sent)
+        copy = lambda: pltpu.make_async_remote_copy(
+            src_ref=src(), dst_ref=dst(), send_sem=ssem.at[at], recv_sem=rsem(),
+            device_id={"z": zz, "b": bb, "col": cc}, device_id_type=MESH,
+        )
+        sent.append((cond, copy))
+        pl.when(cond)(lambda: copy().start())
+
+    def arrived(cond, ref, sem):
+        @pl.when(cond)
+        def _():
+            pltpu.make_async_copy(ref(), ref(), sem()).wait()
+
+    always = z >= 0
+    for t in range(2):
+        own = z == t + 2
+        send(own, lambda: a_ref, lambda t=t: s.at[t, c], lambda t=t: rs.at[t], z - 1, b, c)
+        if t == 0:
+            send(own, lambda: a_ref, lambda: s.at[0, c], lambda: rs.at[0], z + 1, b, c)
+
+        @pl.when(own)
+        def _(t=t):
+            pltpu.make_async_copy(a_ref, s.at[t, c], loc.at[0]).start()
+    for d in range(1, NB):
+        send(always, lambda d=d: f_ref.at[peers[d]], lambda: fi.at[NB * z + b],
+             lambda d=d: rplane.at[d], z, peers[d], c)
+    mine = pltpu.make_async_copy(f_ref.at[b], fi.at[NB * z + b], loc.at[1])
+    mine.start()
+    mine.wait()
+
+    off = lax.rem(z, 2) * 256
+
+    def rows(zz):
+        return pl.ds(NB * zz, NB)
+
+    def piece(zz, cc):
+        lanes = pl.ds(pl.multiple_of(off + 128 * cc, 128), 128)
+        return fi.at[rows(zz), :, lanes]
+
+    def slot(zz, bb):
+        return fj.at[rows(zz), :, pl.ds(pl.multiple_of(bb * 128, 128), 128)]
+
+    def spread_plane(cond, zz, h):
+        take = jnp.logical_and(cond, home)
+        for d in range(NB):
+            for other in range(2):
+                cc = 1 - c if other else c
+                if d == 0 and not other:
+                    @pl.when(take)
+                    def _():
+                        pltpu.make_async_copy(piece(zz, cc), slot(zz, b), loc.at[2 + h]).start()
+                else:
+                    send(take, lambda cc=cc: piece(zz, cc), lambda: slot(zz, b),
+                         lambda: rj.at[b * NB + zz], z, peers[d], cc)
+
+    def spread_rows(cond, t):
+        send(cond, lambda: s.at[t, c], lambda: s.at[t, c], lambda: rsib.at[t], z, b, 1 - c)
+        take = jnp.logical_and(cond, c == 0)
+        low_cols = lambda: s.at[t, 0, :, :, pl.ds(0, 256)]
+        for d in range(1, NB):
+            for cc in range(2):
+                send(take, low_cols, lambda: slo.at[b, t], lambda: rlo.at[b * 2 + t], z, peers[d], cc)
+
+    for d in range(1, NB):
+        arrived(always, lambda d=d: fi.at[NB * z + sources[d]], lambda d=d: rplane.at[d])
+    plane = lambda zz: (lambda: fi.at[rows(zz)])
+    send(high, plane(z), plane(z), lambda: rp.at[z], z + 1, b, c)
+    send(low, plane(z), plane(z), lambda: rp.at[z], z - 1, b, c)
+    spread_plane(always, z, 0)
+    for t in range(2):
+        own = z == t + 2
+
+        @pl.when(own)
+        def _(t=t):
+            pltpu.make_async_copy(a_ref, s.at[t, c], loc.at[0]).wait()
+        spread_rows(own, t)
+    slots = 2
+    for h in range(1, 4):
+        for up in (False, True):
+            zz = z - h if up else z + h
+            here = zz >= 0 if up else zz <= 3
+            on = jnp.logical_and(here, high if up else low)
+            nxt = z + 1 if up else z - 1
+            for t in range(2):
+                got = jnp.logical_and(here, zz == t + 2)
+                if up and (t == 1 or h > 1):
+                    continue
+                arrived(got, lambda t=t: s.at[t, c], lambda t=t: rs.at[t])
+                if not up:
+                    send(jnp.logical_and(got, low), lambda t=t: s.at[t, c], lambda t=t: s.at[t, c],
+                         lambda t=t: rs.at[t], nxt, b, c)
+                spread_rows(got, t)
+            arrived(here, plane(zz), lambda zz=zz: rp.at[zz])
+            send(on, plane(zz), plane(zz), lambda zz=zz: rp.at[zz], nxt, b, c)
+            spread_plane(here, zz, 2 * h - 1 + int(up))
+    for t in range(2):
+        arrived(always, lambda t=t: s.at[t, 1 - c], lambda t=t: rsib.at[t])
+        for d in range(1, NB):
+            arrived(always, lambda d=d, t=t: slo.at[peers[d], t],
+                    lambda d=d, t=t: rlo.at[peers[d] * 2 + t])
+    for zz in range(4):
+        for d in range(NB):
+            cond = always if d else jnp.logical_not(home)
+            arrived(cond, lambda zz=zz, d=d: slot(zz, peers[d]),
+                    lambda zz=zz, d=d: rj.at[peers[d] * NB + zz])
+    for h in range(4):
+        for up in (False, True):
+            if h == 0 and up:
+                continue
+            zz = z if h == 0 else (z - h if up else z + h)
+            here = jnp.logical_and(zz >= 0, zz <= 3)
+
+            @pl.when(jnp.logical_and(here, home))
+            def _(zz=zz, h=h, up=up):
+                sem = loc.at[2 + (2 * h - 1 + int(up) if h else 0)]
+                pltpu.make_async_copy(piece(zz, c), slot(zz, b), sem).wait()
+    for cond, copy in sent:
+        pl.when(cond)(lambda: copy().wait_send())
+
+
+def gather_blocks(f_b, a):
+    any_spec = pl.BlockSpec(memory_space=pl.ANY)
+    f32 = jnp.float32
+    dma = pltpu.SemaphoreType.DMA
+    return pl.pallas_call(
+        gather_kernel,
+        out_shape=(
+            jax.ShapeDtypeStruct((16, BLK, 512), f32),
+            jax.ShapeDtypeStruct((16, BLK, 512), f32),
+            jax.ShapeDtypeStruct((2, 2, 3, BLK, 1024), f32),
+            jax.ShapeDtypeStruct((NB, 2, 3, BLK, 256), f32),
+        ),
+        in_specs=[any_spec] * 2,
+        out_specs=(any_spec,) * 4,
+        scratch_shapes=[
+            dma((9,)), dma((160,)), dma((4,)), dma((NB,)), dma((16,)), dma((2,)), dma((2,)), dma((8,)),
+        ],
+        compiler_params=pltpu.CompilerParams(collective_id=0, has_side_effects=True),
+        name="gather_blocks",
+    )(f_b, a)
+
+
+def grouped_device(root_cov, structure, child_factor, child_diag):
+    z, b, c = lax.axis_index("z"), lax.axis_index("b"), lax.axis_index("col")
+    nz = lax.axis_size("z")
+    depth, width = child_factor.shape
+    k = depth * nz * NB
+    zh = nz // 2
+    sub = width // (zh * NB)
+    hs = sub // 2
     tiles_dev = root_cov.shape[0] // BLK
     col_tiles = root_cov.shape[1] // BLK
     kb = structure.shape[0]
@@ -57,39 +234,34 @@
     half = lax.psum_scatter(picked, "col", scatter_dimension=1, tiled=True)
     first = (z * NB + b) * tiles_dev
     parts = []
-    for j in range(kb):
+    for j in range(2):
         at = structure[j] - first
-        inside = (at >= 0) & (at < tiles_dev)
+        inside = (at >= 0) & (at < tiles_dev) & (c == 0)
         start = jnp.clip(at, 0, tiles_dev - 1) * BLK
-        piece = lax.dynamic_slice(half, (start, 0), (BLK, half.shape[1]))
+        piece = lax.dynamic_slice(half, (start, 0), (BLK, 2 * BLK))
         parts.append(jnp.where(inside, piece, 0.0))
-    full = jnp.concatenate(parts, axis=0)
-    mine = lax.psum_scatter(full, ("z", "b"), scatter_dimension=0, tiled=True)
-    quarter = lax.all_gather(mine, "z", axis=0, tiled=True)
-    return lax.all_gather(quarter, "col", axis=1, tiled=True)
-
-
-def grouped_device(root_cov, structure, child_factor, child_diag):
-    z, b, c = lax.axis_index("z"), lax.axis_index("b"), lax.axis_index("col")
-    nz = lax.axis_size("z")
-    depth, width = child_factor.shape
-    k = depth * nz * NB
-    zh = nz // 2
-    sub = width // (zh * NB)
-    f4 = child_factor.reshape(depth, zh, NB, sub)
-    f_i = lax.all_to_all(f4, "b", split_axis=2, concat_axis=0, tiled=True)
-    f_i = lax.all_gather(f_i.reshape(NB * depth, zh * sub), "z", axis=0, tiled=True)
-    quarter = select_quarter(root_cov, structure, z, b, c)
-    own = lax.dynamic_slice(f_i, (0, (z % zh) * sub), (k, sub))
-    other = lax.ppermute(own, "col", [(0, 1), (1, 0)])
-    own = jnp.where(c == z // zh, own, other)
-    hs = sub // 2
-    own = lax.dynamic_slice(own, (0, c * hs), (k, hs))
-    f_j = lax.all_gather(own, "b", axis=1, tiled=True)
-    x = -jnp.dot(quarter, f_j, precision=HIGH, preferred_element_type=jnp.float32)
-    x3 = x.reshape(nz, depth, NB * hs)
-    x_all = lax.all_gather(x3, "b", axis=1, tiled=False).reshape(k, NB * hs)
-    x_all = lax.all_gather(x_all, "col", axis=0, tiled=False)
+    low_low = lax.psum(jnp.concatenate(parts, axis=0), ("z", "b", "col"))
+    f_b = child_factor.reshape(depth, zh, NB, sub).transpose(2, 0, 1, 3).reshape(NB, depth, zh * sub)
+    f_i, f_j, s, slo = gather_blocks(f_b, half.reshape(tiles_dev, BLK, half.shape[1]))
+    f_i = f_i.reshape(k, zh * sub)
+    f_j = f_j.reshape(k, NB * hs)
+    rows = s.transpose(0, 2, 3, 1, 4).reshape(2 * tiles_dev, BLK, k)
+    place = (structure // 3) % NB * 6 + (structure // 12 - 2) * 3 + structure % 3
+    low_own = s[:, 0, :, :, : 2 * BLK]
+    low_all = jnp.where((lax.iota(jnp.int32, NB) == b)[:, None, None, None, None], low_own[None], slo)
+    col = jnp.minimum(b, 1) * BLK
+    low_all = lax.dynamic_slice_in_dim(low_all.reshape(NB * 6, BLK, 2 * BLK), col, BLK, axis=2)
+    low_row = jnp.take(low_all, place[2:], axis=0, mode="clip").reshape((kb - 2) * BLK, BLK).T
+    low_row = jnp.concatenate([lax.dynamic_slice(low_low, (col, 0), (BLK, 2 * BLK)), low_row], axis=1)
+    spare = jnp.where(b < 2, low_row, rows[0])
+    rows = jnp.concatenate([spare[None], rows[1:]], axis=0).reshape(6 * BLK, k)
+    x = -jnp.dot(rows, f_j, precision=HIGH, preferred_element_type=jnp.float32)
+    x_all = lax.all_gather(x, "b", axis=0, tiled=True).reshape(NB * 6, BLK, NB * hs)
+    place = jnp.concatenate([jnp.array([0, 6], jnp.int32), place[2:]])
+    x_all = jnp.concatenate(
+        [lax.dynamic_slice_in_dim(x_all, place[j], 1, axis=0) for j in range(kb)], axis=0)
+    x3 = lax.dynamic_slice_in_dim(x_all.reshape(nz, NB, depth, NB * hs), b, 1, axis=1)[:, 0]
+    x_all = lax.all_gather(x_all.reshape(k, NB * hs), "col", axis=0, tiled=False)
     out = lax.dot_general(
         x_all, f_i, (((1,), (0,)), ((), ())), precision=HIGH,
         preferred_element_type=jnp.float32,

time: 593 us -> 486 us (0.82)
  waiting for transfers between devices: 386 us -> 68 us
  Pallas kernels: 0 us -> 194 us
  local copies, waits for them, and re-layouts: 30.8 us -> 80.3 us
  blocking collectives: 72.9 us -> 30.2 us
  between operations: 36.3 us -> 55.5 us
  other arithmetic: 39 us -> 27.4 us
    pallas_call x0 -> x1, Pallas kernels: none -> 194 us  [gather_blocks(): pl.pallas_call(gather_kernel, out_shape=(jax.ShapeDtypeStruct((16, BLK, 5...]
    reduce_scatter x2 -> x1, waiting for transfers between devices: 200 us -> 7.89 us  [grouped_device(): half = lax.psum_scatter(picked, 'col', scatter_dimension=1, tiled=True)]
    all_gather x6 -> x2, waiting for transfers between devices: 160 us -> 38.1 us  [the longest x1 38 us: grouped_device(): lax.all_gather(x, 'b', axis=0, tiled=True).reshape(NB * 6, BLK, NB * hs)]
    all_to_all x1 -> x0, blocking collectives: 42.9 us -> none  [grouped_device(): f_i = lax.all_to_all(f4, 'b', split_axis=2, concat_axis=0, tiled=True)]
    unnamed x10 -> x23, local copies, waits for them, and re-layouts: 7.56 us -> 29.6 us
    unnamed x30 -> x15, other arithmetic: 31.2 us -> 14.2 us
    concatenate x0 -> x4, local copies, waits for them, and re-layouts: none -> 9.34 us  [the longest x1 6.66 us: grouped_device(): rows = jnp.concatenate([spare[None], rows[1:]], axis=0).reshape(6 * BLK, k)]
    dot_general x0 -> x1, local copies, waits for them, and re-layouts: none -> 8.69 us  [grouped_device(): lax.dot_general(x_all, f_i, (((1,), (0,)), ((), ())), precision=HIGH, pre...]
  transfers between devices with their start and end apart: 11 -> 6, of which waited for: 8 -> 3; matrix products, arithmetic and copies ran while one was open for 4% -> 9% of each run, Pallas kernels for 0% -> 40%
where the time goes in v2:
time: 486 us; the launch traced here: 484 us
  Pallas kernels  194 us (40%)
  local copies, waits for them, and re-layouts  80.3 us (17%)
  waiting for transfers between devices  68 us (14%)
  between operations  55.5 us (11%)
  blocking collectives  30.2 us (6%)
  other arithmetic  27.4 us (6%)
  matrix products  21.1 us (4%)
  starting transfers between devices  7.53 us (2%)
    pallas_call x1, Pallas kernels, gather_blocks(): pl.pallas_call(gather_kernel, out_shape=(jax.ShapeDtypeStruct((16, BLK, 5...  194 us
    all_gather x1, waiting for transfers between devices, grouped_device(): lax.all_gather(x, 'b', axis=0, tiled=True).reshape(NB * 6, BLK, NB * hs)  38 us
    all_to_all x1, blocking collectives, grouped_device(): y = lax.all_to_all(x3, 'z', split_axis=0, concat_axis=0, tiled=True)  30.2 us
    unnamed x23, local copies, waits for them, and re-layouts  29.6 us
    all_to_all x1, waiting for transfers between devices, grouped_device(): out = lax.all_to_all(out, 'b', split_axis=1, concat_axis=1, tiled=True)  22 us
    unnamed x15, other arithmetic  14.2 us
    dot_general x1, matrix products, grouped_device(): lax.dot_general(x_all, f_i, (((1,), (0,)), ((), ())), precision=HIGH, pre...  11.5 us
  transfers between devices with their start and end apart: 6, of which 3 were waited for; matrix products, arithmetic and copies ran while one was open for 9% of the time, Pallas kernels for 40%

profile of v2, /device:TPU:0, one launch (start us, length us, event | category | flops | bytes accessed | tf_op | source)
XLA Modules:
  0.0 483.7 jit_solution(11534871849948703829)
XLA Ops:
  7.2 2.0 fusion.8
  38.3 1.9 reshape.58
  40.8 1.8 reshape.59.f_ref
  42.6 7.9 %reduce-scatter.2.cloned.1.call-done = f32[384,1024]{1,0:T(8,128)} async-done(((f32[384,2048]{1,0:T(8,128)}), f32[384,1024]{1,0:T(8,128)}) %reduce-scatter.2.cloned.1.call-update) | async-done | bytes 1572880 | tf_op jit(solution)/shard_map/reduce_scatter | solution.py:234
  52.3 193.6 %gather_blocks.1 = (f32[16,128,512]{2,1,0:T(8,128)}, f32[16,128,512]{2,1,0:T(8,128)}, f32[2,2,3,128,1024]{4,3,2,1,0:T(8,128)}, f32[4,2,3,128,256]{4,3,2,1,0:T(8,128)}) custom-call(f32[4,128,512]{2,1,0:T(8,128)} %reshape.59.f_ref, f32[3,128,1024]{2,1,0:T(8,128)} %bitcast.99), custom_call_target="tpu_custom_call" | custom-call | tf_op jit(solution)/shard_map/gather_blocks/pallas_call | solution.py:197
  247.1 6.6 %copy.28 = f32[2,3,128,2,1024]{2,4,3,1,0:T(8,128)} copy(f32[2,3,128,2,1024]{4,2,1,3,0:T(8,128)} %bitcast.75) | data formatting | bytes 12582912 | tf_op jit(solution)/shard_map/transpose | solution.py:248
  253.7 5.2 %slice.164 = f32[5,128,2048]{1,2,0:T(8,128)} slice(f32[6,128,2048]{1,2,0:T(8,128)} %bitcast.70), slice={[1:6], [0:128], [0:2048]} | slice | bytes 10485760 | tf_op jit(solution)/shard_map/slice | solution.py:257
  262.6 5.5 %pad_maximum_fusion = f32[6,128,2048]{1,2,0:T(8,128)} fusion(f32[5,128,2048]{1,2,0:T(8,128)} %slice.164, f32[1,128,2048]{1,2,0:T(8,128)S(1)} %slice_select_fusion), kind=kLoop, calls=%fused_computation.3 | loop fusion | flops 1572864 | bytes 12582912 | tf_op jit(solution)/shard_map/concatenate | solution.py:257
  268.1 6.7 %copy.29 = f32[6,128,2048]{2,1,0:T(8,128)} copy(f32[6,128,2048]{1,2,0:T(8,128)} %pad_maximum_fusion) | data formatting | bytes 12582912 | tf_op jit(solution)/shard_map/concatenate | solution.py:257
  274.7 9.6 %convolution_negate_fusion = f32[768,512]{1,0:T(8,128)} fusion(f32[768,2048]{1,0:T(8,128)} %bitcast.77, f32[2048,512]{1,0:T(8,128)} %bitcast.101), kind=kOutput, calls=%fused_computation.5 | convolution fusion | flops 4832231424 | bytes 12058624 | tf_op jit(solution)/shard_map/dot_general | solution.py:258
  315.3 38.0 %all-gather.3.cloned.1.call-done = f32[3072,512]{1,0:T(8,128)} async-done(((f32[768,512]{1,0:T(8,128)}), f32[3072,512]{1,0:T(8,128)}) %all-gather.3.cloned.1.call-update) | async-done | bytes 6291472 | tf_op jit(solution)/shard_map/all_gather | solution.py:259
  355.0 1.7 dynamic-slice_dynamic-update-slice_fusion.14
  368.4 1.7 dynamic-slice_dynamic-update-slice_fusion.6
  381.8 30.2 %all_to_all.15 = f32[4,128,512]{1,2,0:T(8,128)} all-to-all(f32[4,128,512]{1,2,0:T(8,128)S(1)} %bitcast.80), channel_id=1, replica_groups=mesh['z'=4,'b'=4,'col'=2] {'z'}, dimensions={0} | all-to-all | bytes 2097152 | tf_op jit(solution)/shard_map/all_to_all | solution.py:273
  412.0 3.8 all-to-all-start.1
  415.8 8.7 %copy.32 = f32[2,512,2048]{2,1,0:T(8,128)} copy(f32[2,512,2048]{1,2,0:T(8,128)} %bitcast.72) | data formatting | bytes 16777216 | tf_op jit(solution)/shard_map/dot_general | solution.py:265
  424.5 11.5 %fusion = f32[2,4,128,512]{3,2,0,1:T(8,128)} fusion(f32[2048,512,1,1]{1,0,2,3:T(8,128)} %bitcast.100, f32[2,4,128,2048]{3,2,1,0:T(8,128)} %bitcast.73), kind=kOutput, calls=%fused_computation.1 | convolution fusion | flops 6442450944 | bytes 14680064 | tf_op jit(solution)/shard_map/dot_general | solution.py:265
  435.9 3.6 all-to-all-start.2
  440.6 2.5 copy.35
  443.1 22.0 %all-to-all-done.2 = f32[2,4,128,512]{3,2,0,1:T(8,128)S(1)} async-done(((f32[2,4,128,512]{3,2,0,1:T(8,128)}), f32[2,4,128,512]{3,2,0,1:T(8,128)S(1)}, u32[]{:S(2)}, u32[]{:S(2)}) %all-to-all-start.2) | async-done | bytes 2097184 | tf_op jit(solution)/shard_map/all_to_all | solution.py:270
  465.1 2.3 reshape.71
  467.4 4.3 copy.34
  471.7 2.3 reshape.72
  474.1 3.2 sub.88
  (67 shorter events, 51.6 us)
Async XLA Ops:
  7.2 43.3 %reduce-scatter.2.cloned.1.call-start = ((), (), s32[]{:S(2)}) async-start(), calls=%async_computation.4 | async-start | bytes 4718592 | tf_op jit(solution)/shard_map/reduce_scatter | solution.py:234
  22.6 15.6 %copy-start.2 = (s32[16]{0:T(128)S(1)}, s32[16]{0:T(128)}, u32[]{:S(2)}) copy-start(s32[16]{0:T(128)} %param.6) | copy-start | bytes 196
  35.0 1.7 copy-start
  36.7 223.5 %all-reduce.2.cloned.1.call-start = ((), (), s32[]{:S(2)}) async-start(), calls=%async_computation.5 | async-start | bytes 524288 | tf_op jit(solution)/shard_map/psum | solution.py:243
  52.2 301.1 %all-gather.3.cloned.1.call-start = ((), (), s32[]{:S(2)}) async-start(), calls=%async_computation.6 | async-start | bytes 7864320 | tf_op jit(solution)/shard_map/all_gather | solution.py:259
  253.7 5.3 %copy-start.1 = (f32[4,2,3,128,256]{4,3,2,1,0:T(8,128)S(1)}, f32[4,2,3,128,256]{4,3,2,1,0:T(8,128)}, u32[]{:S(2)}) copy-start(f32[4,2,3,128,256]{4,3,2,1,0:T(8,128)} %get-tuple-element.7) | copy-start | bytes 9437188
  284.4 131.4 %all-gather.5.cloned.1.call-start = ((), (), s32[]{:S(2)}) async-start(), calls=%async_computation.7 | async-start | bytes 12582912 | tf_op jit(solution)/shard_map/all_gather | solution.py:264
  412.0 23.9 %all-to-all-start.1 = ((f32[2,2,128,4,128]{2,4,3,1,0:T(8,128)}), f32[2,2,128,4,128]{2,4,3,1,0:T(8,128)S(1)}, u32[]{:S(2)}, u32[]{:S(2)}) async-start(f32[2,2,128,4,128]{2,4,3,1,0:T(8,128)} %bitcast.47), calls=%async_computation.2 | async-start | bytes 2097152 | tf_op jit(solution)/shard_map/all_to_all | solution.py:275
  435.9 29.2 %all-to-all-start.2 = ((f32[2,4,128,512]{3,2,0,1:T(8,128)}), f32[2,4,128,512]{3,2,0,1:T(8,128)S(1)}, u32[]{:S(2)}, u32[]{:S(2)}) async-start(f32[2,4,128,512]{3,2,0,1:T(8,128)} %fusion), calls=%async_computation.3 | async-start | bytes 4194304 | tf_op jit(solution)/shard_map/all_to_all | solution.py:270
Sparse Core Ops, SparseCore 0:
  36.8 13.6 reduce-scatter.1
  57.5 144.9 all-reduce.1
  284.5 68.7 all-gather.2
  380.2 19.8 all-gather.4

commit v3 on v2

--- a/solution.py
+++ b/solution.py
@@ -45,6 +45,143 @@
     return (cross_cov, child_cov)
 
 
+def select_kernel(at_ref, inside_ref, x_ref, o_ref):
+    o_ref[...] = jnp.where(inside_ref[pl.program_id(0)] > 0, x_ref[...], 0.0)
+
+
+def select_columns(mat, tiles):
+    rows, cols = mat.shape
+    inside = ((tiles >= 0) & (tiles < cols // BLK)).astype(jnp.int32)
+    kb = tiles.shape[0]
+    return pl.pallas_call(
+        select_kernel,
+        out_shape=jax.ShapeDtypeStruct((rows, kb * BLK), mat.dtype),
+        grid_spec=pltpu.PrefetchScalarGridSpec(
+            num_scalar_prefetch=2, grid=(kb,),
+            in_specs=[pl.BlockSpec((rows, BLK), lambda j, at, ok: (0, at[j]))],
+            out_specs=pl.BlockSpec((rows, BLK), lambda j, at, ok: (0, j)),
+        ),
+        name="select_columns",
+    )(jnp.clip(tiles, 0, cols // BLK - 1), inside, mat)
+
+
+def permute_kernel(at_ref, x_ref, o_ref):
+    o_ref[...] = x_ref[...]
+
+
+def permute_tiles(x, place):
+    _, depth, width = x.shape
+    kb = place.shape[0]
+    return pl.pallas_call(
+        permute_kernel,
+        out_shape=jax.ShapeDtypeStruct((kb, depth, width), x.dtype),
+        grid_spec=pltpu.PrefetchScalarGridSpec(
+            num_scalar_prefetch=1, grid=(kb,),
+            in_specs=[pl.BlockSpec((1, depth, width), lambda j, at: (at[j], 0, 0))],
+            out_specs=pl.BlockSpec((1, depth, width), lambda j, at: (j, 0, 0)),
+        ),
+        name="permute_tiles",
+    )(place, x)
+
+
+def scatter_kernel(o_ref, x_ref, res, y, loc, ssem, rres, ry):
+    z, b, c = lax.axis_index("z"), lax.axis_index("b"), lax.axis_index("col")
+    home = c == z // 2
+    away = jnp.logical_not(home)
+    peers = [lax.rem(b + d, NB) for d in range(NB)]
+    sources = [lax.rem(b + NB - d, NB) for d in range(NB)]
+    planes = [lax.rem(z + d, 4) for d in range(4)]
+    barrier = pltpu.get_barrier_semaphore()
+
+    def greet(zz, bb, cc):
+        pl.semaphore_signal(
+            barrier, inc=1, device_id={"z": zz, "b": bb, "col": cc}, device_id_type=MESH
+        )
+
+    for d in range(1, NB):
+        greet(z, peers[d], c)
+        greet(planes[d], b, c)
+    for d in range(4):
+        greet(planes[d], b, 1 - c)
+    pl.semaphore_wait(barrier, 10)
+
+    def block(bb, zi):
+        return pl.ds(pl.multiple_of(zi * 1024 + bb * 256, 128), 256)
+
+    def lanes(zi, bb, cc):
+        return pl.ds(pl.multiple_of(zi * 1024 + bb * 256 + cc * 128, 128), 128)
+
+    always = z >= 0
+    sent, local = [], []
+
+    def send(cond, src, dst, rsem, zz, bb, cc):
+        copy = pltpu.make_async_remote_copy(
+            src_ref=src, dst_ref=dst, send_sem=ssem.at[len(sent)], recv_sem=rsem,
+            device_id={"z": zz, "b": bb, "col": cc}, device_id_type=MESH,
+        )
+        sent.append((cond, copy))
+        pl.when(cond)(lambda: copy.start())
+
+    def keep(cond, src, dst):
+        copy = pltpu.make_async_copy(src, dst, loc.at[len(local)])
+        local.append((cond, copy))
+        pl.when(cond)(lambda: copy.start())
+
+    for d in range(1, NB):
+        for q in range(2):
+            for zi in range(2):
+                send(always, o_ref.at[q, peers[d], :, pl.ds(zi * 256, 256)], res.at[q, :, block(b, zi)],
+                     rres.at[4 * d + 2 * q + zi], z, peers[d], c)
+    zpar = lax.rem(z, 2)
+    for d in range(4):
+        for bb in range(NB):
+            src = x_ref.at[planes[d], :, pl.ds(bb * 128, 128)]
+            dst = y.at[:, lanes(zpar, bb, c)]
+            if d == 0:
+                keep(home, src, dst)
+                send(away, src, dst, ry.at[(2 * z + c) * NB + bb], z, b, 1 - c)
+            else:
+                send(always, src, dst, ry.at[(2 * z + c) * NB + bb], planes[d], b, z // 2)
+    for q in range(2):
+        for zi in range(2):
+            keep(always, o_ref.at[q, b, :, pl.ds(zi * 256, 256)], res.at[q, :, block(b, zi)])
+
+    for d in range(1, NB):
+        for q in range(2):
+            for zi in range(2):
+                ref = res.at[q, :, block(sources[d], zi)]
+                pltpu.make_async_copy(ref, ref, rres.at[4 * d + 2 * q + zi]).wait()
+    for zi in range(2):
+        for cc in range(2):
+            zz = 2 * c + zi
+            other = jnp.logical_or(zz != z, c != cc)
+            for bb in range(NB):
+                ref = y.at[:, lanes(zi, bb, cc)]
+                copy = pltpu.make_async_copy(ref, ref, ry.at[(2 * zz + cc) * NB + bb])
+                pl.when(other)(lambda copy=copy: copy.wait())
+    for cond, copy in local:
+        pl.when(cond)(lambda copy=copy: copy.wait())
+    for cond, copy in sent:
+        pl.when(cond)(lambda copy=copy: copy.wait_send())
+
+
+def scatter_blocks(out, x3):
+    any_spec = pl.BlockSpec(memory_space=pl.ANY)
+    dma = pltpu.SemaphoreType.DMA
+    return pl.pallas_call(
+        scatter_kernel,
+        out_shape=(
+            jax.ShapeDtypeStruct((2, BLK, 2048), jnp.float32),
+            jax.ShapeDtypeStruct((BLK, 2048), jnp.float32),
+        ),
+        in_specs=[any_spec] * 2,
+        out_specs=(any_spec,) * 2,
+        scratch_shapes=[dma((8,)), dma((28,)), dma((16,)), dma((32,))],
+        compiler_params=pltpu.CompilerParams(collective_id=1, has_side_effects=True),
+        name="scatter_blocks",
+    )(out, x3)
+
+
 def gather_kernel(f_ref, a_ref, fi, fj, s, slo, loc, ssem, rp, rplane, rj, rs, rsib, rlo):
     z, b, c = lax.axis_index("z"), lax.axis_index("b"), lax.axis_index("col")
     low, high = z > 0, z < 3
@@ -68,6 +205,9 @@
     pl.semaphore_wait(barrier, 2 * NB - 1 + low.astype(jnp.int32) + high.astype(jnp.int32))
 
     sent = []
+
+    def rows_half(t, cc):
+        return s.at[t, :, :, pl.ds(pl.multiple_of(cc * 1024, 128), 1024)]
 
     def send(cond, src, dst, rsem, zz, bb, cc):
         at = len(sent)
@@ -86,13 +226,13 @@
     always = z >= 0
     for t in range(2):
         own = z == t + 2
-        send(own, lambda: a_ref, lambda t=t: s.at[t, c], lambda t=t: rs.at[t], z - 1, b, c)
+        send(own, lambda: a_ref, lambda t=t: rows_half(t, c), lambda t=t: rs.at[t], z - 1, b, c)
         if t == 0:
-            send(own, lambda: a_ref, lambda: s.at[0, c], lambda: rs.at[0], z + 1, b, c)
+            send(own, lambda: a_ref, lambda: rows_half(0, c), lambda: rs.at[0], z + 1, b, c)
 
         @pl.when(own)
         def _(t=t):
-            pltpu.make_async_copy(a_ref, s.at[t, c], loc.at[0]).start()
+            pltpu.make_async_copy(a_ref, rows_half(t, c), loc.at[0]).start()
     for d in range(1, NB):
         send(always, lambda d=d: f_ref.at[peers[d]], lambda: fi.at[NB * z + b],
              lambda d=d: rplane.at[d], z, peers[d], c)
@@ -126,9 +266,9 @@
                          lambda: rj.at[b * NB + zz], z, peers[d], cc)
 
     def spread_rows(cond, t):
-        send(cond, lambda: s.at[t, c], lambda: s.at[t, c], lambda: rsib.at[t], z, b, 1 - c)
+        send(cond, lambda: rows_half(t, c), lambda: rows_half(t, c), lambda: rsib.at[t], z, b, 1 - c)
         take = jnp.logical_and(cond, c == 0)
-        low_cols = lambda: s.at[t, 0, :, :, pl.ds(0, 256)]
+        low_cols = lambda: s.at[t, :, :, pl.ds(0, 256)]
         for d in range(1, NB):
             for cc in range(2):
                 send(take, low_cols, lambda: slo.at[b, t], lambda: rlo.at[b * 2 + t], z, peers[d], cc)
@@ -144,7 +284,7 @@
 
         @pl.when(own)
         def _(t=t):
-            pltpu.make_async_copy(a_ref, s.at[t, c], loc.at[0]).wait()
+            pltpu.make_async_copy(a_ref, rows_half(t, c), loc.at[0]).wait()
         spread_rows(own, t)
     slots = 2
     for h in range(1, 4):
@@ -157,16 +297,16 @@
                 got = jnp.logical_and(here, zz == t + 2)
                 if up and (t == 1 or h > 1):
                     continue
-                arrived(got, lambda t=t: s.at[t, c], lambda t=t: rs.at[t])
+                arrived(got, lambda t=t: rows_half(t, c), lambda t=t: rs.at[t])
                 if not up:
-                    send(jnp.logical_and(got, low), lambda t=t: s.at[t, c], lambda t=t: s.at[t, c],
+                    send(jnp.logical_and(got, low), lambda t=t: rows_half(t, c), lambda t=t: rows_half(t, c),
                          lambda t=t: rs.at[t], nxt, b, c)
                 spread_rows(got, t)
             arrived(here, plane(zz), lambda zz=zz: rp.at[zz])
             send(on, plane(zz), plane(zz), lambda zz=zz: rp.at[zz], nxt, b, c)
             spread_plane(here, zz, 2 * h - 1 + int(up))
     for t in range(2):
-        arrived(always, lambda t=t: s.at[t, 1 - c], lambda t=t: rsib.at[t])
+        arrived(always, lambda t=t: rows_half(t, 1 - c), lambda t=t: rsib.at[t])
         for d in range(1, NB):
             arrived(always, lambda d=d, t=t: slo.at[peers[d], t],
                     lambda d=d, t=t: rlo.at[peers[d] * 2 + t])
@@ -199,7 +339,7 @@
         out_shape=(
             jax.ShapeDtypeStruct((16, BLK, 512), f32),
             jax.ShapeDtypeStruct((16, BLK, 512), f32),
-            jax.ShapeDtypeStruct((2, 2, 3, BLK, 1024), f32),
+            jax.ShapeDtypeStruct((2, 3, BLK, 2048), f32),
             jax.ShapeDtypeStruct((NB, 2, 3, BLK, 256), f32),
         ),
         in_specs=[any_spec] * 2,
@@ -223,14 +363,7 @@
     tiles_dev = root_cov.shape[0] // BLK
     col_tiles = root_cov.shape[1] // BLK
     kb = structure.shape[0]
-    parts = []
-    for j in range(kb):
-        at = structure[j] - c * col_tiles
-        inside = (at >= 0) & (at < col_tiles)
-        start = jnp.clip(at, 0, col_tiles - 1) * BLK
-        piece = lax.dynamic_slice(root_cov, (0, start), (root_cov.shape[0], BLK))
-        parts.append(jnp.where(inside, piece, 0.0))
-    picked = jnp.concatenate(parts, axis=1)
+    picked = select_columns(root_cov, structure - c * col_tiles)
     half = lax.psum_scatter(picked, "col", scatter_dimension=1, tiled=True)
     first = (z * NB + b) * tiles_dev
     parts = []
@@ -245,36 +378,28 @@
     f_i, f_j, s, slo = gather_blocks(f_b, half.reshape(tiles_dev, BLK, half.shape[1]))
     f_i = f_i.reshape(k, zh * sub)
     f_j = f_j.reshape(k, NB * hs)
-    rows = s.transpose(0, 2, 3, 1, 4).reshape(2 * tiles_dev, BLK, k)
+    rows = s.reshape(2 * tiles_dev, BLK, k)
     place = (structure // 3) % NB * 6 + (structure // 12 - 2) * 3 + structure % 3
-    low_own = s[:, 0, :, :, : 2 * BLK]
+    low_own = s[..., : 2 * BLK]
     low_all = jnp.where((lax.iota(jnp.int32, NB) == b)[:, None, None, None, None], low_own[None], slo)
     col = jnp.minimum(b, 1) * BLK
     low_all = lax.dynamic_slice_in_dim(low_all.reshape(NB * 6, BLK, 2 * BLK), col, BLK, axis=2)
     low_row = jnp.take(low_all, place[2:], axis=0, mode="clip").reshape((kb - 2) * BLK, BLK).T
     low_row = jnp.concatenate([lax.dynamic_slice(low_low, (col, 0), (BLK, 2 * BLK)), low_row], axis=1)
     spare = jnp.where(b < 2, low_row, rows[0])
-    rows = jnp.concatenate([spare[None], rows[1:]], axis=0).reshape(6 * BLK, k)
+    rows = lax.dynamic_update_slice(rows, spare[None], (0, 0, 0)).reshape(6 * BLK, k)
     x = -jnp.dot(rows, f_j, precision=HIGH, preferred_element_type=jnp.float32)
     x_all = lax.all_gather(x, "b", axis=0, tiled=True).reshape(NB * 6, BLK, NB * hs)
     place = jnp.concatenate([jnp.array([0, 6], jnp.int32), place[2:]])
-    x_all = jnp.concatenate(
-        [lax.dynamic_slice_in_dim(x_all, place[j], 1, axis=0) for j in range(kb)], axis=0)
+    x_all = permute_tiles(x_all, place)
     x3 = lax.dynamic_slice_in_dim(x_all.reshape(nz, NB, depth, NB * hs), b, 1, axis=1)[:, 0]
     x_all = lax.all_gather(x_all.reshape(k, NB * hs), "col", axis=0, tiled=False)
     out = lax.dot_general(
         x_all, f_i, (((1,), (0,)), ((), ())), precision=HIGH,
         preferred_element_type=jnp.float32,
     )
-    out = out.reshape(2, NB, hs, zh * sub)
-    out = lax.all_to_all(out, "b", split_axis=1, concat_axis=1, tiled=True)
-    out = out.reshape(2, NB, hs, zh, sub).transpose(0, 2, 3, 1, 4).reshape(2 * hs, width)
-    child_cov = child_diag - out
-    y = lax.all_to_all(x3, "z", split_axis=0, concat_axis=0, tiled=True)
-    y = y.reshape(2, zh, depth, NB, hs)
-    y = lax.all_to_all(y, "col", split_axis=0, concat_axis=0, tiled=True)
-    cross_cov = y.transpose(2, 1, 3, 0, 4).reshape(depth, width)
-    return (cross_cov, child_cov)
+    child, cross_cov = scatter_blocks(out.reshape(2, NB, hs, zh * sub), x3)
+    return (cross_cov, child_diag - child.reshape(2 * hs, width))
 
 
 def solution(mesh):

time: 486 us -> 408 us (0.84)
  local copies, waits for them, and re-layouts: 80.3 us -> 18.8 us
  Pallas kernels: 194 us -> 242 us
  between operations: 55.5 us -> 15.2 us
  blocking collectives: 30.2 us -> 0 us
  waiting for transfers between devices: 68 us -> 96.8 us
  other arithmetic: 27.4 us -> 12.5 us
  starting transfers between devices: 7.53 us -> 0.34 us
    pallas_call x0 -> x3, Pallas kernels: none -> 48.6 us  [the longest x1 29.7 us: scatter_blocks(): pl.pallas_call(scatter_kernel, out_shape=(jax.ShapeDtypeStruct((2, BLK, 2...]
    all_to_all x1 -> x0, blocking collectives: 30.2 us -> none  [grouped_device(): y = lax.all_to_all(x3, 'z', split_axis=0, concat_axis=0, tiled=True)]
    all_gather x1, waiting for transfers between devices: 38 us -> 68.1 us  [grouped_device(): lax.all_gather(x, 'b', axis=0, tiled=True).reshape(NB * 6, BLK, NB * hs)]
    unnamed x23 -> x9, local copies, waits for them, and re-layouts: 29.6 us -> 0.99 us
    all_to_all x2 -> x0, waiting for transfers between devices: 22 us -> none  [the longest x1 22 us: grouped_device(): out = lax.all_to_all(out, 'b', split_axis=1, concat_axis=1, tiled=True)]
    all_gather x1, waiting for transfers between devices: 0.02 us -> 17.7 us  [grouped_device(): lax.all_gather(x_all.reshape(k, NB * hs), 'col', axis=0, tiled=False)]
    unnamed x15 -> x0, other arithmetic: 14.2 us -> none
    transpose x3 -> x0, local copies, waits for them, and re-layouts: 11.9 us -> none  [the longest x1 6.58 us: grouped_device(): rows = s.transpose(0, 2, 3, 1, 4).reshape(2 * tiles_dev, BLK, k)]
  transfers between devices with their start and end apart: 6 -> 4, of which waited for: 3 -> 3; matrix products, arithmetic and copies ran while one was open for 9% -> 3% of each run, Pallas kernels for 40% -> 48%
where the time goes in v3:
time: 408 us; the launch traced here: 407 us
  Pallas kernels  242 us (59%)
  waiting for transfers between devices  96.8 us (24%)
  matrix products  21.1 us (5%)
  local copies, waits for them, and re-layouts  18.8 us (5%)
  between operations  15.2 us (4%)
  other arithmetic  12.5 us (3%)
    pallas_call x1, Pallas kernels, gather_blocks(): pl.pallas_call(gather_kernel, out_shape=(jax.ShapeDtypeStruct((16, BLK, 5...  194 us
    all_gather x1, waiting for transfers between devices, grouped_device(): lax.all_gather(x, 'b', axis=0, tiled=True).reshape(NB * 6, BLK, NB * hs)  68.1 us
    pallas_call x1, Pallas kernels, scatter_blocks(): pl.pallas_call(scatter_kernel, out_shape=(jax.ShapeDtypeStruct((2, BLK, 2...  29.7 us
    all_gather x1, waiting for transfers between devices, grouped_device(): lax.all_gather(x_all.reshape(k, NB * hs), 'col', axis=0, tiled=False)  17.7 us
    dot_general x1, matrix products, grouped_device(): lax.dot_general(x_all, f_i, (((1,), (0,)), ((), ())), precision=HIGH, pre...  11.5 us
    reduce_scatter x1, waiting for transfers between devices, grouped_device(): half = lax.psum_scatter(picked, 'col', scatter_dimension=1, tiled=True)  10.9 us
    pallas_call x1, Pallas kernels, permute_tiles(): pl.pallas_call(permute_kernel, out_shape=jax.ShapeDtypeStruct((kb, depth,...  10.8 us
    dot_general x1, matrix products, grouped_device(): x = -jnp.dot(rows, f_j, precision=HIGH, preferred_element_type=jnp.float32)  9.64 us
  transfers between devices with their start and end apart: 4, of which 3 were waited for; matrix products, arithmetic and copies ran while one was open for 3% of the time, Pallas kernels for 48%

profile of v3, /device:TPU:0, one launch (start us, length us, event | category | flops | bytes accessed | tf_op | source)
XLA Modules:
  0.0 407.1 jit_solution(2925062189056670177)
XLA Ops:
  7.2 1.2 and_convert_fusion.inside_ref
  8.4 1.2 subtract_clamp_fusion
  9.6 8.1 %select_columns.1 = f32[384,2048]{1,0:T(8,128)} custom-call(s32[16]{0:T(128)} %get-tuple-element.18.at_ref, s32[16]{0:T(128)} %and_convert_fusion.inside_ref, f32[384,3072]{1,0:T(8,128)} %x_ref.1), custom_call_target="tpu_custom_call" | custom-call | tf_op jit(solution)/shard_map/select_columns/pallas_call | solution.py:56
  19.7 0.7 reshape.49
  21.0 1.8 reshape.50.f_ref
  22.8 10.9 %reduce-scatter.2.cloned.1.call-done = f32[384,1024]{1,0:T(8,128)} async-done(((f32[384,2048]{1,0:T(8,128)}), f32[384,1024]{1,0:T(8,128)}) %reduce-scatter.2.cloned.1.call-update) | async-done | bytes 1572880 | tf_op jit(solution)/shard_map/reduce_scatter | solution.py:367
  33.7 1.0 dynamic-slice_select_fusion.1
  34.7 0.7 pad_maximum_fusion
  35.5 193.7 %gather_blocks.1 = (f32[16,128,512]{2,1,0:T(8,128)}, f32[16,128,512]{2,1,0:T(8,128)}, f32[2,3,128,2048]{3,2,1,0:T(8,128)}, f32[4,2,3,128,256]{4,3,2,1,0:T(8,128)}) custom-call(f32[4,128,512]{2,1,0:T(8,128)} %reshape.50.f_ref, f32[3,128,1024]{2,1,0:T(8,128)} %bitcast.45), custom_call_target="tpu_custom_call" | custom-call | tf_op jit(solution)/shard_map/gather_blocks/pallas_call | solution.py:337
  229.2 1.2 slice.19
  230.4 2.3 broadcast_select_fusion
  232.8 0.6 gather_fusion
  233.7 0.9 dynamic-slice_bitcast_fusion.1
  234.7 2.3 fusion
  237.0 9.6 %convolution_negate_fusion = f32[768,512]{1,0:T(8,128)} fusion(f32[768,2048]{1,0:T(8,128)} %bitcast.47, f32[2048,512]{1,0:T(8,128)} %bitcast.49), kind=kOutput, calls=%fused_computation.3 | convolution fusion | flops 4832231424 | bytes 12058624 | tf_op jit(solution)/shard_map/dot_general | solution.py:391
  247.5 68.1 %all-gather.3.cloned.1.call-done = f32[3072,512]{1,0:T(8,128)} async-done(((f32[768,512]{1,0:T(8,128)}), f32[3072,512]{1,0:T(8,128)}) %all-gather.3.cloned.1.call-update) | async-done | bytes 6291472 | tf_op jit(solution)/shard_map/all_gather | solution.py:392
  315.6 10.8 %permute_tiles.1 = f32[16,128,512]{2,1,0:T(8,128)} custom-call(s32[16]{0:T(128)} %pad_add_fusion.at_ref, f32[24,128,512]{2,1,0:T(8,128)} %bitcast.41), custom_call_target="tpu_custom_call" | custom-call | tf_op jit(solution)/shard_map/permute_tiles/pallas_call | solution.py:75
  326.4 2.3 dynamic-slice_bitcast_fusion.x_ref
  328.7 17.7 %all-gather.5.cloned.1.call-done = f32[2,2048,512]{2,1,0:T(8,128)} async-done(((f32[1,2048,512]{2,1,0:T(8,128)}), f32[2,2048,512]{2,1,0:T(8,128)}) %all-gather.5.cloned.1.call-update) | async-done | bytes 8388624 | tf_op jit(solution)/shard_map/all_gather | solution.py:396
  346.5 8.7 %copy.13 = f32[2,512,2048]{2,1,0:T(8,128)} copy(f32[2,512,2048]{1,2,0:T(8,128)} %bitcast.38) | data formatting | bytes 16777216 | tf_op jit(solution)/shard_map/dot_general | solution.py:397
  355.2 11.5 %fusion.6.o_ref = f32[2,4,128,512]{3,2,1,0:T(8,128)} fusion(f32[2,4,128,2048]{3,2,1,0:T(8,128)} %bitcast.39, f32[2048,512,1,1]{1,0,3,2:T(8,128)} %bitcast.48), kind=kOutput, calls=%fused_computation.30 | convolution fusion | flops 6442450944 | bytes 14680064 | tf_op jit(solution)/shard_map/dot_general | solution.py:397
  366.6 29.7 %scatter_blocks.1 = (f32[2,128,2048]{2,1,0:T(8,128)}, f32[128,2048]{1,0:T(8,128)}) custom-call(f32[2,4,128,512]{3,2,1,0:T(8,128)} %fusion.6.o_ref, f32[4,128,512]{2,1,0:T(8,128)} %dynamic-slice_bitcast_fusion.x_ref), custom_call_target="tpu_custom_call" | custom-call | tf_op jit(solution)/shard_map/scatter_blocks/pallas_call | solution.py:171
  396.4 3.2 bitcast_subtract_fusion
  399.6 1.0 copy.22
  (26 shorter events, 2.7 us)
Async XLA Ops:
  7.2 26.6 %reduce-scatter.2.cloned.1.call-start = ((), (), s32[]{:S(2)}) async-start(), calls=%async_computation.1 | async-start | bytes 4718592 | tf_op jit(solution)/shard_map/reduce_scatter | solution.py:367
  9.6 8.2 %copy-start.3 = (s32[16]{0:T(128)S(1)}, s32[16]{0:T(128)}, u32[]{:S(2)}) copy-start(s32[16]{0:T(128)} %param.6) | copy-start | bytes 196
  9.6 10.2 %copy-start.1 = (f32[128,2048]{1,0:T(8,128)S(1)}, f32[128,2048]{1,0:T(8,128)}, u32[]{:S(2)}) copy-start(f32[128,2048]{1,0:T(8,128)} %param.7) | copy-start | bytes 3145732
  17.7 216.1 %all-reduce.2.cloned.1.call-start = ((), (), s32[]{:S(2)}) async-start(), calls=%async_computation.2 | async-start | bytes 524288 | tf_op jit(solution)/shard_map/psum | solution.py:376
  35.5 280.1 %all-gather.3.cloned.1.call-start = ((), (), s32[]{:S(2)}) async-start(), calls=%async_computation.3 | async-start | bytes 7864320 | tf_op jit(solution)/shard_map/all_gather | solution.py:392
  246.7 99.8 %all-gather.5.cloned.1.call-start = ((), (), s32[]{:S(2)}) async-start(), calls=%async_computation.4 | async-start | bytes 12582912 | tf_op jit(solution)/shard_map/all_gather | solution.py:396
  366.6 29.7 %copy-start = (f32[256,2048]{1,0:T(8,128)S(1)}, f32[256,2048]{1,0:T(8,128)}, u32[]{:S(2)}) copy-start(f32[256,2048]{1,0:T(8,128)} %param.8) | copy-start | bytes 6291460
  396.4 3.3 copy-start.2
Sparse Core Ops, SparseCore 0:
  17.8 15.8 reduce-scatter.1
  40.7 144.8 all-reduce.1
  246.8 68.7 all-gather.2
  326.6 19.8 all-gather.4
